TPU v7x, 512 devices: a whole 4x8x8 slice. The times are simulated.
512 devices in a mesh: dp: 128 (over y, z, core), group: 4 (over x).
Axes of the slice: x: 4, y: 8, z: 8, core: 2. Of those that a mesh axis runs over, the one named last changes fastest.
Arguments:
- gradient: float32 [176, 1024, 768], P(None, ('dp', 'group')), may hold values from -90 to 90
- momentum: float32 [176, 1024, 768], P(None, ('dp', 'group')), may hold values from -90 to 90
- weight: bfloat16 [176, 1024, 768], P(None, ('dp', 'group')), may hold values from -0.21875 to 0.21875
Outputs:
- new_momentum: float32 [176, 1024, 768], P(None, ('dp', 'group'))
- update: bfloat16 [176, 1024, 768], P(None, ('dp', 'group'))
- new_weight: bfloat16 [176, 1024, 768], P(None, ('dp', 'group'))
All inputs are finite; a program needn't handle non-finite values.
Results may differ from a plain program's by a relative error of at most 0.0088.
Values may be sent and summed in bfloat16 or wider, within the bound.
A program may use at most 64 MiB of HBM per device.

v0:
```python
import math

import jax
import jax.numpy as jnp
from jax import lax
from jax.sharding import PartitionSpec as P

ROWS = 1024
COLS = 768
ITERS = 2


momentum_decay = 0.95
coef_first = 3.4445
coef_second = -4.775
coef_third = 2.0315
epsilon_norm = 1e-07
learning_rate = 0.02
weight_decay = 0.1
rms_match = 0.2


def orthogonalize(matrix):
    values = matrix.astype(jnp.float32)
    frobenius = jnp.sqrt(jnp.sum(values * values))
    current = (values / (frobenius + epsilon_norm)).astype(jnp.bfloat16)
    for iteration in range(ITERS):
        gram_matrix = lax.dot_general(
            current, current, (((0,), (0,)), ((), ())), preferred_element_type=jnp.float32
        ).astype(jnp.bfloat16)
        squared = jnp.dot(gram_matrix, gram_matrix, preferred_element_type=jnp.float32)
        polynomial = (coef_second * gram_matrix.astype(jnp.float32) + coef_third * squared).astype(
            jnp.bfloat16
        )
        current = (
            coef_first * current.astype(jnp.float32)
            + jnp.dot(current, polynomial, preferred_element_type=jnp.float32)
        ).astype(jnp.bfloat16)
    return current


def per_device(gradient, momentum, weight):
    matrix_count, local_rows, column_count = gradient.shape
    dp_count = lax.axis_size("dp")
    group_count = lax.axis_size("group")
    new_momentum = momentum_decay * momentum + gradient
    advance = (gradient + momentum_decay * new_momentum).astype(jnp.bfloat16)
    slot_count = dp_count * group_count
    padded = jnp.pad(advance, ((0, slot_count - matrix_count), (0, 0), (0, 0)))
    outgoing = padded.reshape(dp_count, group_count, 1, 1, local_rows, column_count)
    arrived = lax.all_to_all(
        lax.all_to_all(outgoing, "dp", split_axis=0, concat_axis=2, tiled=True),
        "group",
        split_axis=1,
        concat_axis=3,
        tiled=True,
    )
    finished = orthogonalize(arrived.reshape(-1, column_count))
    returned = lax.all_to_all(
        lax.all_to_all(
            finished.reshape(1, 1, dp_count, group_count, local_rows, column_count),
            "dp",
            split_axis=2,
            concat_axis=0,
            tiled=True,
        ),
        "group",
        split_axis=3,
        concat_axis=1,
        tiled=True,
    )
    orthogonal = returned.reshape(slot_count, local_rows, column_count)[:matrix_count]
    factor = rms_match * math.sqrt(max(ROWS, COLS))
    update = (factor * orthogonal.astype(jnp.float32)).astype(jnp.bfloat16)
    new_weight = (
        (1.0 - learning_rate * weight_decay) * weight.astype(jnp.float32)
        - learning_rate * update.astype(jnp.float32)
    ).astype(jnp.bfloat16)
    return (new_momentum, update, new_weight)


def solution(mesh):
    return jax.shard_map(
        per_device,
        mesh=mesh,
        in_specs=(
            P(None, ("dp", "group"), None),
            P(None, ("dp", "group"), None),
            P(None, ("dp", "group"), None),
        ),
        out_specs=(
            P(None, ("dp", "group"), None),
            P(None, ("dp", "group"), None),
            P(None, ("dp", "group"), None),
        ),
        check_vma=False,
    )
```

profile of v0, /device:TPU:1, one launch (start us, length us, event | category | flops | bytes accessed | tf_op | source)
XLA Modules:
  0.0 183.9 jit_solution(16715217001715863549)
XLA Ops:
  0.6 3.7 %add_convert_fusion.4 = (bf16[176,2,768]{2,1,0:T(2,128)(2,1)S(1)}, f32[176,2,768]{2,1,0:T(2,128)}) fusion(f32[176,2,768]{2,1,0:T(2,128)} %param.3, f32[176,2,768]{2,1,0:T(2,128)} %param.4), kind=kLoop, calls=%fused_computation.13 | loop fusion | flops 1351680 | bytes 3784704 | tf_op jit(solution)/shard_map/convert_element_type | solution.py:47
  4.3 0.9 pad.4
  5.2 59.3 %all_to_all.48 = bf16[128,4,1,1,2,768]{5,4,1,3,2,0:T(2,128)(2,1)S(1)} all-to-all(bf16[128,4,1,1,2,768]{5,4,1,3,2,0:T(2,128)(2,1)S(1)} %bitcast.42), channel_id=1, replica_groups=mesh['dp'=128,'group'=4] {'dp'}, dimensions={0} | all-to-all | bytes 3145728 | tf_op jit(solution)/shard_map/all_to_all | solution.py:52
  64.5 0.3 copy.26
  64.8 22.9 %all_to_all.49 = bf16[1,4,128,1,2,768]{5,2,4,3,0,1:T(8,128)(2,1)S(1)} all-to-all(bf16[1,4,128,1,2,768]{5,2,4,3,0,1:T(8,128)(2,1)S(1)} %copy.26), channel_id=1, replica_groups=mesh['dp'=128,'group'=4] {'group'}, dimensions={1} | all-to-all | bytes 3145728 | tf_op jit(solution)/shard_map/all_to_all | solution.py:51
  87.7 1.4 fusion
  89.8 0.3 fusion.8
  90.1 1.6 copy.28
  91.7 1.5 convert_element_type.78
  93.3 2.5 %bitcast_convert_fusion = bf16[768,768]{1,0:T(8,128)(2,1)} fusion(bf16[1,4,128,1,2,768]{5,2,4,3,0,1:T(8,128)(2,1)S(1)} %all_to_all.49, f32[]{:T(128)S(6)} %add.25), kind=kOutput, calls=%fused_computation.6 | convolution fusion | flops 1210908672 | bytes 2752516 | tf_op jit(solution)/shard_map/dot_general | solution.py:28
  95.7 0.0 copy-done.1
  95.7 4.6 %add_convert_fusion.1 = bf16[1024,768]{1,0:T(8,128)(2,1)S(1)} fusion(bf16[1024,768]{1,0:T(8,128)(2,1)S(1)} %copy-done.1, bf16[768,768]{1,0:T(8,128)(2,1)} %bitcast_convert_fusion), kind=kOutput, calls=%fused_computation.5 | convolution fusion | flops 2120024064 | bytes 4325376 | tf_op jit(solution)/shard_map/dot_general | solution.py:37
  100.3 2.5 %convolution_convert_fusion = bf16[768,768]{1,0:T(8,128)(2,1)} fusion(bf16[1024,768]{1,0:T(8,128)(2,1)S(1)} %add_convert_fusion.1), kind=kOutput, calls=%fused_computation.10 | convolution fusion | flops 1208549376 | bytes 2752512 | tf_op jit(solution)/shard_map/dot_general | solution.py:28
  102.7 4.5 %add_convert_fusion = bf16[1024,768]{1,0:T(8,128)(2,1)S(1)} fusion(bf16[1024,768]{1,0:T(8,128)(2,1)S(1)} %add_convert_fusion.1, bf16[768,768]{1,0:T(8,128)(2,1)} %convolution_convert_fusion), kind=kOutput, calls=%fused_computation.4 | convolution fusion | flops 2120024064 | bytes 4325376 | tf_op jit(solution)/shard_map/dot_general | solution.py:37
  107.2 0.6 reshape.49
  107.9 50.5 %all_to_all.50 = bf16[1,1,128,4,2,768]{5,4,3,1,0,2:T(2,128)(2,1)S(1)} all-to-all(bf16[1,1,128,4,2,768]{5,4,3,1,0,2:T(2,128)(2,1)S(1)} %bitcast.44), channel_id=1, replica_groups=mesh['dp'=128,'group'=4] {'dp'}, dimensions={2} | all-to-all | bytes 3145728 | tf_op jit(solution)/shard_map/all_to_all | solution.py:60
  158.4 1.1 copy.31
  159.5 21.5 %all_to_all.51 = bf16[128,1,1,4,2,768]{5,4,0,2,1,3:T(2,128)(2,1)S(1)} all-to-all(bf16[128,1,1,4,2,768]{5,4,0,2,1,3:T(2,128)(2,1)S(1)} %copy.31), channel_id=1, replica_groups=mesh['dp'=128,'group'=4] {'group'}, dimensions={3} | all-to-all | bytes 3145728 | tf_op jit(solution)/shard_map/all_to_all | solution.py:59
  181.0 0.4 slice.6
  181.4 0.3 multiply_convert_fusion
  181.6 0.4 copy.33
  182.1 0.0 copy-done.2
  182.1 0.0 copy-start
  182.1 1.8 subtract_convert_fusion
  (3 shorter events, 0.0 us)
Async XLA Ops:
  93.2 2.5 %copy-start.1 = (bf16[1024,768]{1,0:T(8,128)(2,1)S(1)}, bf16[1024,768]{1,0:T(8,128)(2,1)}, u32[]{:S(2)}) copy-start(bf16[1024,768]{1,0:T(8,128)(2,1)} %convert_element_type.78) | copy-start | bytes 4718596
  181.0 1.1 copy-start.2
  182.1 1.8 copy-start
where the time goes:
time: 185 us; the launch traced here: 184 us
  blocking collectives  154 us (83%)
  matrix products  14 us (8%)
  other arithmetic  7.4 us (4%)
  local copies, waits for them, and re-layouts  6.89 us (4%)
    all_to_all x1, blocking collectives, per_device(): lax.all_to_all(outgoing, 'dp', split_axis=0, concat_axis=2, tiled=True)  59.3 us
    all_to_all x1, blocking collectives, per_device(): lax.all_to_all(finished.reshape(1, 1, dp_count, group_count, local_rows,...  50.5 us
    all_to_all x1, blocking collectives, per_device(): lax.all_to_all(lax.all_to_all(outgoing, 'dp', split_axis=0, concat_axis=2...  22.9 us
    all_to_all x1, blocking collectives, per_device(): lax.all_to_all(lax.all_to_all(finished.reshape(1, 1, dp_count, group_coun...  21.5 us
    dot_general x2, matrix products, orthogonalize(): jnp.dot(current, polynomial, preferred_element_type=jnp.float32)  9.04 us
    dot_general x2, matrix products, orthogonalize(): lax.dot_general(current, current, (((0,), (0,)), ((), ())), preferred_ele...  4.93 us

commit v1 on v0

v1 whole, which is shorter than its diff:
```python
import math

import jax
import jax.numpy as jnp
from jax import lax
from jax.experimental import pallas as pl
from jax.experimental.pallas import tpu as pltpu
from jax.sharding import PartitionSpec as P

ROWS = 1024
COLS = 768
ITERS = 2
MATS = 176
DEVICES = 512

momentum_decay = 0.95
coef_first = 3.4445
coef_second = -4.775
coef_third = 2.0315
epsilon_norm = 1e-07
learning_rate = 0.02
weight_decay = 0.1
rms_match = 0.2

MESH = pl.DeviceIdType.MESH
TILE = 256
STEP = 16


def owner_of(t):
    x = lax.rem(t, 4)
    r = lax.div(t, 4)
    pair = lax.div(r, 11)
    k = lax.rem(r, 11)
    six = k < 6
    kk = jnp.where(six, k, k - 6)
    parity = lax.rem(x, 2)
    y = 2 * pair + jnp.where(six, parity, 1 - parity)
    skip = jnp.where(jnp.logical_and(jnp.logical_not(six), kk >= 4), 1, 0)
    d = kk + 1 + jnp.where(kk >= 2, 1, 0) + skip
    z = lax.rem(y + d + 2 * x, 8)
    return (y * 8 + z) * 2, x


def matrix_of(dp, x):
    core = lax.rem(dp, 2)
    place = lax.div(dp, 2)
    y = lax.div(place, 8)
    z = lax.rem(place, 8)
    d = lax.rem(z - y - 2 * x + 16, 8)
    six = lax.rem(y, 2) == lax.rem(x, 2)
    gap = jnp.logical_or(d == 0, d == 3)
    gap = jnp.logical_or(gap, jnp.logical_and(jnp.logical_not(six), d == 6))
    owns = jnp.logical_and(core == 0, jnp.logical_not(gap))
    kk = d - 1 - jnp.where(d >= 4, 1, 0)
    kk = kk - jnp.where(jnp.logical_and(jnp.logical_not(six), d >= 7), 1, 0)
    k = jnp.where(six, kk, kk + 6)
    t = (lax.div(y, 2) * 11 + k) * 4 + x
    return owns, jnp.where(owns, t, 0)


def dot_first(a, b):
    return lax.dot_general(a, b, (((0,), (0,)), ((), ())), preferred_element_type=jnp.float32)


def kernel(
    gradient, momentum, weight,
    new_momentum, update, new_weight,
    g_buf, m_buf, w_buf, nm_buf, advance, arrived, current, after, gram, poly, finished, returned, nw_buf,
    load_sem, store_sem, own_sem, send_sem, recv_sem, back_send, back_recv,
):
    dp = lax.axis_index("dp")
    x = lax.axis_index("group")
    me = dp * 4 + x
    owns, mine = matrix_of(dp, x)
    barrier = pltpu.get_barrier_semaphore()

    @pl.when(owns)
    def _():
        @pl.loop(1, DEVICES)
        def _(j):
            r = lax.rem(me + j, DEVICES)
            pl.semaphore_signal(barrier, inc=1, device_id=(lax.div(r, 4), lax.rem(r, 4)), device_id_type=MESH)

    loads = [
        pltpu.make_async_copy(gradient, g_buf, load_sem.at[0]),
        pltpu.make_async_copy(momentum, m_buf, load_sem.at[1]),
        pltpu.make_async_copy(weight, w_buf, load_sem.at[2]),
    ]
    for c in loads:
        c.start()
    for c in loads:
        c.wait()

    def mix(i, _):
        s = pl.ds(pl.multiple_of(i * STEP, STEP), STEP)
        g = g_buf[s]
        nm = momentum_decay * m_buf[s] + g
        nm_buf[s] = nm
        advance[s] = (g + momentum_decay * nm).astype(jnp.bfloat16)
        return 0

    lax.fori_loop(0, MATS // STEP, mix, 0)
    keep_momentum = pltpu.make_async_copy(nm_buf, new_momentum, store_sem.at[0])
    keep_momentum.start()

    own_count = jnp.where(owns, 1, 0)
    pl.semaphore_wait(barrier, MATS - own_count)

    shift = dp * 7 + x * 44

    @pl.loop(0, MATS)
    def _(k):
        t = lax.rem(k + shift, MATS)
        there = owner_of(t)

        @pl.when(jnp.logical_or(there[0] != dp, there[1] != x))
        def _():
            pltpu.make_async_remote_copy(
                src_ref=advance.at[t], dst_ref=arrived.at[me], send_sem=send_sem, recv_sem=recv_sem,
                device_id=there, device_id_type=MESH,
            ).start()

    @pl.when(owns)
    def _():
        own = pltpu.make_async_copy(advance.at[mine], arrived.at[me], own_sem.at[0])
        own.start()
        own.wait()
        pltpu.make_async_copy(
            arrived.at[pl.ds(0, DEVICES - 1)], arrived.at[pl.ds(0, DEVICES - 1)], recv_sem
        ).wait()

        def gather(i, total):
            block = arrived[pl.ds(pl.multiple_of(i * 32, 32), 32)].reshape(64, COLS)
            current[pl.ds(pl.multiple_of(i * 64, 64), 64), :] = block
            v = block.astype(jnp.float32)
            return total + jnp.sum(v * v)

        total = lax.fori_loop(0, DEVICES // 32, gather, jnp.float32(0))
        norm = jnp.sqrt(jnp.full((1, 1), total, jnp.float32)) + epsilon_norm

        def scale(i, _):
            s = pl.ds(pl.multiple_of(i * 64, 64), 64)
            current[s, :] = (current[s, :].astype(jnp.float32) / norm).astype(jnp.bfloat16)
            return 0

        lax.fori_loop(0, ROWS // 64, scale, 0)

        def make_poly(source):
            for j in range(COLS // TILE):
                c = slice(j * TILE, (j + 1) * TILE)
                gram[:, c] = dot_first(source[...], source[:, c]).astype(jnp.bfloat16)
            for j in range(COLS // TILE):
                c = slice(j * TILE, (j + 1) * TILE)
                squared = jnp.dot(gram[...], gram[:, c], preferred_element_type=jnp.float32)
                poly[:, c] = (coef_second * gram[:, c].astype(jnp.float32) + coef_third * squared).astype(
                    jnp.bfloat16
                )

        make_poly(current)
        for i in range(ROWS // TILE):
            r = slice(i * TILE, (i + 1) * TILE)
            product = jnp.dot(current[r, :], poly[...], preferred_element_type=jnp.float32)
            after[r, :] = (coef_first * current[r, :].astype(jnp.float32) + product).astype(jnp.bfloat16)
        make_poly(after)
        factor = rms_match * math.sqrt(max(ROWS, COLS))

        def finish(i, _):
            plane = lax.rem(i + lax.div(dp, 16), 8)
            r = pl.ds(pl.multiple_of(plane * 128, 128), 128)
            rows = after[r, :]
            product = jnp.dot(rows, poly[...], preferred_element_type=jnp.float32)
            rows = (coef_first * rows.astype(jnp.float32) + product).astype(jnp.bfloat16)
            rows = (factor * rows.astype(jnp.float32)).astype(jnp.bfloat16)
            finished[pl.ds(pl.multiple_of(plane * 64, 64), 64)] = rows.reshape(64, 2, COLS)

            @pl.loop(0, 64)
            def _(k):
                to = plane * 64 + lax.rem(me + k * 5, 64)

                @pl.when(to != me)
                def _():
                    pltpu.make_async_remote_copy(
                        src_ref=finished.at[to], dst_ref=returned.at[mine],
                        send_sem=back_send, recv_sem=back_recv,
                        device_id=(lax.div(to, 4), lax.rem(to, 4)), device_id_type=MESH,
                    ).start()

            return 0

        lax.fori_loop(0, 8, finish, 0)
        own_back = pltpu.make_async_copy(finished.at[me], returned.at[mine], own_sem.at[1])
        own_back.start()
        own_back.wait()
        pltpu.make_async_copy(
            advance.at[pl.ds(0, MATS - 1)], advance.at[pl.ds(0, MATS - 1)], send_sem
        ).wait()
        pltpu.make_async_copy(
            returned.at[pl.ds(0, MATS - 1)], returned.at[pl.ds(0, MATS - 1)], back_recv
        ).wait()
        pltpu.make_async_copy(
            finished.at[pl.ds(0, DEVICES - 1)], finished.at[pl.ds(0, DEVICES - 1)], back_send
        ).wait()

    @pl.when(jnp.logical_not(owns))
    def _():
        pltpu.make_async_copy(advance, advance, send_sem).wait()
        pltpu.make_async_copy(returned, returned, back_recv).wait()

    keep_update = pltpu.make_async_copy(returned, update, store_sem.at[1])
    keep_update.start()

    def step(i, _):
        s = pl.ds(pl.multiple_of(i * STEP, STEP), STEP)
        nw_buf[s] = (
            (1.0 - learning_rate * weight_decay) * w_buf[s].astype(jnp.float32)
            - learning_rate * returned[s].astype(jnp.float32)
        ).astype(jnp.bfloat16)
        return 0

    lax.fori_loop(0, MATS // STEP, step, 0)
    keep_weight = pltpu.make_async_copy(nw_buf, new_weight, store_sem.at[2])
    keep_weight.start()
    keep_momentum.wait()
    keep_update.wait()
    keep_weight.wait()


def per_device(gradient, momentum, weight):
    shape = gradient.shape
    f32, bf16 = jnp.float32, jnp.bfloat16
    blocks = (DEVICES,) + shape[1:]
    return pl.pallas_call(
        kernel,
        out_shape=(
            jax.ShapeDtypeStruct(shape, f32),
            jax.ShapeDtypeStruct(shape, bf16),
            jax.ShapeDtypeStruct(shape, bf16),
        ),
        in_specs=[pl.BlockSpec(memory_space=pl.ANY)] * 3,
        out_specs=[pl.BlockSpec(memory_space=pl.ANY)] * 3,
        scratch_shapes=[
            pltpu.VMEM(shape, f32),
            pltpu.VMEM(shape, f32),
            pltpu.VMEM(shape, bf16),
            pltpu.VMEM(shape, f32),
            pltpu.VMEM(shape, bf16),
            pltpu.VMEM(blocks, bf16),
            pltpu.VMEM((ROWS, COLS), bf16),
            pltpu.VMEM((ROWS, COLS), bf16),
            pltpu.VMEM((COLS, COLS), bf16),
            pltpu.VMEM((COLS, COLS), bf16),
            pltpu.VMEM(blocks, bf16),
            pltpu.VMEM(shape, bf16),
            pltpu.VMEM(shape, bf16),
            pltpu.SemaphoreType.DMA((3,)),
            pltpu.SemaphoreType.DMA((3,)),
            pltpu.SemaphoreType.DMA((2,)),
            pltpu.SemaphoreType.DMA,
            pltpu.SemaphoreType.DMA,
            pltpu.SemaphoreType.DMA,
            pltpu.SemaphoreType.DMA,
        ],
        compiler_params=pltpu.CompilerParams(
            collective_id=0, has_side_effects=True, vmem_limit_bytes=48 * 2**20
        ),
    )(gradient, momentum, weight)


def solution(mesh):
    spec = P(None, ("dp", "group"), None)
    return jax.shard_map(
        per_device, mesh=mesh, in_specs=(spec, spec, spec), out_specs=(spec, spec, spec), check_vma=False
    )
```

time: 185 us -> 88.5 us (0.48)
  blocking collectives: 154 us -> 0 us
  Pallas kernels: 0 us -> 81.5 us
  matrix products: 14 us -> 0 us
  other arithmetic: 7.4 us -> 0 us
    all_to_all x4 -> x0, blocking collectives: 154 us -> none  [the longest x1 59.3 us: per_device(): lax.all_to_all(outgoing, 'dp', split_axis=0, concat_axis=2, tiled=True)]
    pallas_call x0 -> x1, Pallas kernels: none -> 81.5 us  [per_device(): pl.pallas_call(kernel, out_shape=(jax.ShapeDtypeStruct(shape, f32), jax.S...]
    dot_general x4 -> x0, matrix products: 14 us -> none  [the longest x2 9.04 us: orthogonalize(): jnp.dot(current, polynomial, preferred_element_type=jnp.float32)]
    unnamed x6 -> x9, local copies, waits for them, and re-layouts: 0.01 us -> 6.09 us
    convert_element_type x4 -> x0, other arithmetic: 6 us -> none  [the longest x1 3.65 us: per_device(): advance = (gradient + momentum_decay * new_momentum).astype(jnp.bfloat16)]
    convert_element_type x3 -> x0, local copies, waits for them, and re-layouts: 3.56 us -> none  [the longest x2 3.14 us: orthogonalize(): current = (values / (frobenius + epsilon_norm)).astype(jnp.bfloat16)]
where the time goes in v1:
time: 88.5 us; the launch traced here: 88.3 us
  Pallas kernels  81.5 us (92%)
  local copies, waits for them, and re-layouts  6.09 us (7%)
    pallas_call x1, Pallas kernels, per_device(): pl.pallas_call(kernel, out_shape=(jax.ShapeDtypeStruct(shape, f32), jax.S...  81.5 us
    unnamed x9, local copies, waits for them, and re-layouts  6.09 us

profile of v1, /device:TPU:1, one launch (start us, length us, event | category | flops | bytes accessed | tf_op | source)
XLA Modules:
  0.0 88.3 jit_solution(12979595480786278591)
XLA Ops:
  0.6 0.0 copy-start
  0.6 1.2 %copy-done = f32[176,2,768]{2,1,0:T(2,128)S(1)} copy-done((f32[176,2,768]{2,1,0:T(2,128)S(1)}, f32[176,2,768]{2,1,0:T(2,128)}, u32[]{:S(2)}) %copy-start) | copy-done | bytes 1081368
  1.9 0.0 copy-start.1
  1.9 1.2 %copy-done.1 = f32[176,2,768]{2,1,0:T(2,128)S(1)} copy-done((f32[176,2,768]{2,1,0:T(2,128)S(1)}, f32[176,2,768]{2,1,0:T(2,128)}, u32[]{:S(2)}) %copy-start.1) | copy-done | bytes 1081368
  3.1 0.0 copy-start.2
  3.1 1.0 %copy-done.2 = bf16[176,2,768]{2,1,0:T(2,128)(2,1)S(1)} copy-done((bf16[176,2,768]{2,1,0:T(2,128)(2,1)S(1)}, bf16[176,2,768]{2,1,0:T(2,128)(2,1)}, u32[]{:S(2)}) %copy-start.2) | copy-done | bytes 540696
  4.2 81.5 %shard_map.58 = (f32[176,2,768]{2,1,0:T(2,128)S(1)}, bf16[176,2,768]{2,1,0:T(2,128)(2,1)S(1)}, bf16[176,2,768]{2,1,0:T(2,128)(2,1)S(1)}) custom-call(f32[176,2,768]{2,1,0:T(2,128)S(1)} %copy-done, f32[176,2,768]{2,1,0:T(2,128)S(1)} %copy-done.1, bf16[176,2,768]{2,1,0:T(2,128)(2,1)S(1)} %copy-done.2), custom_call_target="tpu_custom_call" | custom-call | tf_op jit(solution)/shard_map/pallas_call | solution.py:233
  85.7 1.0 %copy.9 = f32[176,2,768]{2,1,0:T(2,128)} copy(f32[176,2,768]{2,1,0:T(2,128)S(1)} %get-tuple-element.6) | data formatting | bytes 2162688
  86.7 0.8 copy.10
  87.5 0.8 copy.11
Async XLA Ops:
  0.6 1.2 %copy-start = (f32[176,2,768]{2,1,0:T(2,128)S(1)}, f32[176,2,768]{2,1,0:T(2,128)}, u32[]{:S(2)}) copy-start(f32[176,2,768]{2,1,0:T(2,128)} %gradient.1) | copy-start | bytes 3244036
  1.9 1.2 %copy-start.1 = (f32[176,2,768]{2,1,0:T(2,128)S(1)}, f32[176,2,768]{2,1,0:T(2,128)}, u32[]{:S(2)}) copy-start(f32[176,2,768]{2,1,0:T(2,128)} %momentum.1) | copy-start | bytes 3244036
  3.1 1.0 %copy-start.2 = (bf16[176,2,768]{2,1,0:T(2,128)(2,1)S(1)}, bf16[176,2,768]{2,1,0:T(2,128)(2,1)}, u32[]{:S(2)}) copy-start(bf16[176,2,768]{2,1,0:T(2,128)(2,1)} %weight.1) | copy-start | bytes 1622020

commit v2 on v1

--- a/solution.py
+++ b/solution.py
@@ -25,19 +25,20 @@
 MESH = pl.DeviceIdType.MESH
 TILE = 256
 STEP = 16
-
-
-def owner_of(t):
-    x = lax.rem(t, 4)
-    r = lax.div(t, 4)
-    pair = lax.div(r, 11)
-    k = lax.rem(r, 11)
+FAR = (4, 3, 5, 2, 6, 1, 7, 0)
+
+
+def offset_of(k):
     six = k < 6
     kk = jnp.where(six, k, k - 6)
+    last = jnp.logical_and(jnp.logical_not(six), kk >= 4)
+    return six, kk + 1 + jnp.where(kk >= 2, 1, 0) + jnp.where(last, 1, 0)
+
+
+def owner_of(q, six, d):
+    x = lax.div(q, 4)
     parity = lax.rem(x, 2)
-    y = 2 * pair + jnp.where(six, parity, 1 - parity)
-    skip = jnp.where(jnp.logical_and(jnp.logical_not(six), kk >= 4), 1, 0)
-    d = kk + 1 + jnp.where(kk >= 2, 1, 0) + skip
+    y = 2 * lax.rem(q, 4) + jnp.where(six, parity, 1 - parity)
     z = lax.rem(y + d + 2 * x, 8)
     return (y * 8 + z) * 2, x
 
@@ -55,19 +56,58 @@
     kk = d - 1 - jnp.where(d >= 4, 1, 0)
     kk = kk - jnp.where(jnp.logical_and(jnp.logical_not(six), d >= 7), 1, 0)
     k = jnp.where(six, kk, kk + 6)
-    t = (lax.div(y, 2) * 11 + k) * 4 + x
+    t = k * 16 + x * 4 + lax.div(y, 2)
     return owns, jnp.where(owns, t, 0)
+
+
+def far_first(a):
+    half = lax.div(a, 2)
+    return jnp.where(lax.rem(a, 2) == 0, 4 - half, lax.rem(5 + half, 8))
 
 
 def dot_first(a, b):
     return lax.dot_general(a, b, (((0,), (0,)), ((), ())), preferred_element_type=jnp.float32)
+
+
+def make_gram(source, gram, norm):
+    scale = None
+    blocks = []
+    for i in range(COLS // TILE):
+        a = i * TILE
+        blocks.append(dot_first(source[:, a : a + TILE], source[:, a:]))
+    if norm:
+        row = lax.broadcasted_iota(jnp.int32, (TILE, TILE), 0)
+        column = lax.broadcasted_iota(jnp.int32, (TILE, TILE), 1)
+        trace = jnp.zeros((1, 1), jnp.float32)
+        for block in blocks:
+            diagonal = jnp.where(row == column, block[:, :TILE], 0.0)
+            trace = trace + jnp.sum(diagonal, axis=(0, 1), keepdims=True)
+        scale = 1.0 / (jnp.sqrt(trace) + epsilon_norm)
+        blocks = [(block * scale) * scale for block in blocks]
+    for i, block in enumerate(blocks):
+        a = i * TILE
+        block = block.astype(jnp.bfloat16)
+        gram[a : a + TILE, a:] = block
+        for j in range(i + 1, COLS // TILE):
+            gram[j * TILE : (j + 1) * TILE, a : a + TILE] = block[:, (j - i) * TILE : (j - i + 1) * TILE].T
+    return scale
+
+
+def make_poly(gram, poly):
+    for i in range(COLS // TILE):
+        a = i * TILE
+        squared = jnp.dot(gram[a : a + TILE, :], gram[:, a:], preferred_element_type=jnp.float32)
+        block = (coef_second * gram[a : a + TILE, a:].astype(jnp.float32) + coef_third * squared).astype(jnp.bfloat16)
+        poly[a : a + TILE, a:] = block
+        for j in range(i + 1, COLS // TILE):
+            poly[j * TILE : (j + 1) * TILE, a : a + TILE] = block[:, (j - i) * TILE : (j - i + 1) * TILE].T
 
 
 def kernel(
     gradient, momentum, weight,
     new_momentum, update, new_weight,
     g_buf, m_buf, w_buf, nm_buf, advance, arrived, current, after, gram, poly, finished, returned, nw_buf,
-    load_sem, store_sem, own_sem, send_sem, recv_sem, back_send, back_recv,
+    ready, load_sem, store_sem, own_sem, send_sem, recv_sem, back_send, back_recv,
 ):
     dp = lax.axis_index("dp")
     x = lax.axis_index("group")
@@ -75,12 +115,9 @@
     owns, mine = matrix_of(dp, x)
     barrier = pltpu.get_barrier_semaphore()
 
-    @pl.when(owns)
-    def _():
-        @pl.loop(1, DEVICES)
-        def _(j):
-            r = lax.rem(me + j, DEVICES)
-            pl.semaphore_signal(barrier, inc=1, device_id=(lax.div(r, 4), lax.rem(r, 4)), device_id_type=MESH)
+    place = lax.div(dp, 2)
+    core = lax.rem(dp, 2)
+    y, z = lax.div(place, 8), lax.rem(place, 8)
 
     loads = [
         pltpu.make_async_copy(gradient, g_buf, load_sem.at[0]),
@@ -89,6 +126,31 @@
     ]
     for c in loads:
         c.start()
+    @pl.when(core == 1)
+    def _():
+        pl.semaphore_signal(barrier, inc=1, device_id=(dp - 1, x), device_id_type=MESH)
+
+    @pl.when(owns)
+    def _():
+        planes = [lax.rem(y + dy, 8) * 16 for dy in FAR]
+        groups = [lax.rem(x + dx, 4) for dx in (2, 1, 3, 0)]
+
+        @pl.loop(0, 8)
+        def _(j):
+            along = lax.rem(z + far_first(j), 8) * 2
+            for plane in planes:
+                for tx in groups:
+                    if plane is planes[-1] and tx is groups[-1]:
+
+                        @pl.when(j != 7)
+                        def _():
+                            pl.semaphore_signal(
+                                barrier, inc=1, device_id=(plane + along, tx), device_id_type=MESH
+                            )
+
+                    else:
+                        pl.semaphore_signal(barrier, inc=1, device_id=(plane + along, tx), device_id_type=MESH)
+
     for c in loads:
         c.wait()
 
@@ -105,21 +167,40 @@
     keep_momentum.start()
 
     own_count = jnp.where(owns, 1, 0)
-    pl.semaphore_wait(barrier, MATS - own_count)
-
-    shift = dp * 7 + x * 44
-
-    @pl.loop(0, MATS)
-    def _(k):
-        t = lax.rem(k + shift, MATS)
-        there = owner_of(t)
-
-        @pl.when(jnp.logical_or(there[0] != dp, there[1] != x))
-        def _():
-            pltpu.make_async_remote_copy(
-                src_ref=advance.at[t], dst_ref=arrived.at[me], send_sem=send_sem, recv_sem=recv_sem,
-                device_id=there, device_id_type=MESH,
-            ).start()
+    @pl.when(core == 0)
+    def _():
+        pl.semaphore_wait(barrier, MATS + 1 - own_count)
+        pl.semaphore_signal(ready, inc=1, device_id=(dp + 1, x), device_id_type=MESH)
+
+    @pl.when(core == 1)
+    def _():
+        pl.semaphore_wait(ready, 1)
+
+    def send_to(count, first, turn):
+        @pl.loop(0, count)
+        def _(i):
+            k = first + 2 * lax.rem(i + turn, count)
+            six, d = offset_of(k)
+            odd = jnp.where(six, 0, 1)
+            for tx in range(4):
+                ty = 1 - odd if tx % 2 else odd
+                tz = lax.rem(ty + d + 2 * tx, 8)
+                for pair in range(4):
+                    there = ((2 * pair + ty) * 8 + tz) * 2
+                    t = k * 16 + tx * 4 + pair
+
+                    @pl.when(jnp.logical_or(there != dp, x != tx))
+                    def _():
+                        pltpu.make_async_remote_copy(
+                            src_ref=advance.at[t], dst_ref=arrived.at[me], send_sem=send_sem, recv_sem=recv_sem,
+                            device_id=(there, tx), device_id_type=MESH,
+                        ).start()
+
+                    tz = tz + 2
+                    tz = jnp.where(tz >= 8, tz - 8, tz)
+
+    send_to(6, 0, z)
+    send_to(5, 1, z)
 
     @pl.when(owns)
     def _():
@@ -130,43 +211,26 @@
             arrived.at[pl.ds(0, DEVICES - 1)], arrived.at[pl.ds(0, DEVICES - 1)], recv_sem
         ).wait()
 
-        def gather(i, total):
+        def gather(i, _):
             block = arrived[pl.ds(pl.multiple_of(i * 32, 32), 32)].reshape(64, COLS)
             current[pl.ds(pl.multiple_of(i * 64, 64), 64), :] = block
-            v = block.astype(jnp.float32)
-            return total + jnp.sum(v * v)
-
-        total = lax.fori_loop(0, DEVICES // 32, gather, jnp.float32(0))
-        norm = jnp.sqrt(jnp.full((1, 1), total, jnp.float32)) + epsilon_norm
-
-        def scale(i, _):
-            s = pl.ds(pl.multiple_of(i * 64, 64), 64)
-            current[s, :] = (current[s, :].astype(jnp.float32) / norm).astype(jnp.bfloat16)
             return 0
 
-        lax.fori_loop(0, ROWS // 64, scale, 0)
-
-        def make_poly(source):
-            for j in range(COLS // TILE):
-                c = slice(j * TILE, (j + 1) * TILE)
-                gram[:, c] = dot_first(source[...], source[:, c]).astype(jnp.bfloat16)
-            for j in range(COLS // TILE):
-                c = slice(j * TILE, (j + 1) * TILE)
-                squared = jnp.dot(gram[...], gram[:, c], preferred_element_type=jnp.float32)
-                poly[:, c] = (coef_second * gram[:, c].astype(jnp.float32) + coef_third * squared).astype(
-                    jnp.bfloat16
-                )
-
-        make_poly(current)
+        lax.fori_loop(0, DEVICES // 32, gather, 0)
+        scale = make_gram(current, gram, True)
+        make_poly(gram, poly)
         for i in range(ROWS // TILE):
             r = slice(i * TILE, (i + 1) * TILE)
             product = jnp.dot(current[r, :], poly[...], preferred_element_type=jnp.float32)
-            after[r, :] = (coef_first * current[r, :].astype(jnp.float32) + product).astype(jnp.bfloat16)
-        make_poly(after)
+            after[r, :] = (scale * (coef_first * current[r, :].astype(jnp.float32) + product)).astype(jnp.bfloat16)
+        make_gram(after, gram, False)
+        make_poly(gram, poly)
         factor = rms_match * math.sqrt(max(ROWS, COLS))
 
+        groups = [lax.rem(x + dx, 4) for dx in (2, 1, 3, 0)]
+
         def finish(i, _):
-            plane = lax.rem(i + lax.div(dp, 16), 8)
+            plane = lax.rem(y + far_first(i), 8)
             r = pl.ds(pl.multiple_of(plane * 128, 128), 128)
             rows = after[r, :]
             product = jnp.dot(rows, poly[...], preferred_element_type=jnp.float32)
@@ -174,17 +238,19 @@
             rows = (factor * rows.astype(jnp.float32)).astype(jnp.bfloat16)
             finished[pl.ds(pl.multiple_of(plane * 64, 64), 64)] = rows.reshape(64, 2, COLS)
 
-            @pl.loop(0, 64)
-            def _(k):
-                to = plane * 64 + lax.rem(me + k * 5, 64)
-
-                @pl.when(to != me)
-                def _():
-                    pltpu.make_async_remote_copy(
-                        src_ref=finished.at[to], dst_ref=returned.at[mine],
-                        send_sem=back_send, recv_sem=back_recv,
-                        device_id=(lax.div(to, 4), lax.rem(to, 4)), device_id_type=MESH,
-                    ).start()
+            @pl.loop(0, 8)
+            def _(j):
+                there = (plane * 8 + lax.rem(z + far_first(j), 8)) * 2
+                for way in range(8):
+                    tx = groups[way % 4]
+                    td = there + way // 4
+
+                    @pl.when(jnp.logical_or(td != dp, tx != x))
+                    def _():
+                        pltpu.make_async_remote_copy(
+                            src_ref=finished.at[td * 4 + tx], dst_ref=returned.at[mine],
+                            send_sem=back_send, recv_sem=back_recv, device_id=(td, tx), device_id_type=MESH,
+                        ).start()
 
             return 0
 
@@ -237,7 +303,7 @@
             jax.ShapeDtypeStruct(shape, bf16),
             jax.ShapeDtypeStruct(shape, bf16),
         ),
-        in_specs=[pl.BlockSpec(memory_space=pl.ANY)] * 3,
+        in_specs=[pl.BlockSpec(memory_space=pltpu.HBM)] * 3,
         out_specs=[pl.BlockSpec(memory_space=pl.ANY)] * 3,
         scratch_shapes=[
             pltpu.VMEM(shape, f32),
@@ -253,6 +319,7 @@
             pltpu.VMEM(blocks, bf16),
             pltpu.VMEM(shape, bf16),
             pltpu.VMEM(shape, bf16),
+            pltpu.SemaphoreType.REGULAR,
             pltpu.SemaphoreType.DMA((3,)),
             pltpu.SemaphoreType.DMA((3,)),
             pltpu.SemaphoreType.DMA((2,)),

time: 88.5 us -> 70.2 us (0.79)
  Pallas kernels: 81.5 us -> 63.2 us
    pallas_call x1, Pallas kernels: 81.5 us -> 63.2 us  [per_device(): pl.pallas_call(kernel, out_shape=(jax.ShapeDtypeStruct(shape, f32), jax.S...]
where the time goes in v2:
time: 70.2 us; the launch traced here: 69.9 us
  Pallas kernels  63.2 us (90%)
  local copies, waits for them, and re-layouts  6.09 us (9%)
    pallas_call x1, Pallas kernels, per_device(): pl.pallas_call(kernel, out_shape=(jax.ShapeDtypeStruct(shape, f32), jax.S...  63.2 us
    unnamed x9, local copies, waits for them, and re-layouts  6.09 us

profile of v2, /device:TPU:1, one launch (start us, length us, event | category | flops | bytes accessed | tf_op | source)
XLA Modules:
  0.0 69.9 jit_solution(1468521986156804349)
XLA Ops:
  0.6 0.0 copy-start
  0.6 1.2 %copy-done = f32[176,2,768]{2,1,0:T(2,128)S(1)} copy-done((f32[176,2,768]{2,1,0:T(2,128)S(1)}, f32[176,2,768]{2,1,0:T(2,128)}, u32[]{:S(2)}) %copy-start) | copy-done | bytes 1081368
  1.9 0.0 copy-start.1
  1.9 1.2 %copy-done.1 = f32[176,2,768]{2,1,0:T(2,128)S(1)} copy-done((f32[176,2,768]{2,1,0:T(2,128)S(1)}, f32[176,2,768]{2,1,0:T(2,128)}, u32[]{:S(2)}) %copy-start.1) | copy-done | bytes 1081368
  3.1 0.0 copy-start.2
  3.1 1.0 %copy-done.2 = bf16[176,2,768]{2,1,0:T(2,128)(2,1)S(1)} copy-done((bf16[176,2,768]{2,1,0:T(2,128)(2,1)S(1)}, bf16[176,2,768]{2,1,0:T(2,128)(2,1)}, u32[]{:S(2)}) %copy-start.2) | copy-done | bytes 540696
  4.2 63.2 %shard_map.58 = (f32[176,2,768]{2,1,0:T(2,128)S(1)}, bf16[176,2,768]{2,1,0:T(2,128)(2,1)S(1)}, bf16[176,2,768]{2,1,0:T(2,128)(2,1)S(1)}) custom-call(f32[176,2,768]{2,1,0:T(2,128)S(1)} %copy-done, f32[176,2,768]{2,1,0:T(2,128)S(1)} %copy-done.1, bf16[176,2,768]{2,1,0:T(2,128)(2,1)S(1)} %copy-done.2), custom_call_target="tpu_custom_call" | custom-call | tf_op jit(solution)/shard_map/pallas_call | solution.py:299
  67.3 1.0 %copy.9 = f32[176,2,768]{2,1,0:T(2,128)} copy(f32[176,2,768]{2,1,0:T(2,128)S(1)} %get-tuple-element.6) | data formatting | bytes 2162688
  68.3 0.8 %copy.10 = bf16[176,2,768]{2,1,0:T(2,128)(2,1)} copy(bf16[176,2,768]{2,1,0:T(2,128)(2,1)S(1)} %get-tuple-element.7) | data formatting | bytes 1081344
  69.1 0.8 %copy.11 = bf16[176,2,768]{2,1,0:T(2,128)(2,1)} copy(bf16[176,2,768]{2,1,0:T(2,128)(2,1)S(1)} %get-tuple-element.8) | data formatting | bytes 1081344
Async XLA Ops:
  0.6 1.2 %copy-start = (f32[176,2,768]{2,1,0:T(2,128)S(1)}, f32[176,2,768]{2,1,0:T(2,128)}, u32[]{:S(2)}) copy-start(f32[176,2,768]{2,1,0:T(2,128)} %gradient.1) | copy-start | bytes 3244036
  1.9 1.2 %copy-start.1 = (f32[176,2,768]{2,1,0:T(2,128)S(1)}, f32[176,2,768]{2,1,0:T(2,128)}, u32[]{:S(2)}) copy-start(f32[176,2,768]{2,1,0:T(2,128)} %momentum.1) | copy-start | bytes 3244036
  3.1 1.0 %copy-start.2 = (bf16[176,2,768]{2,1,0:T(2,128)(2,1)S(1)}, bf16[176,2,768]{2,1,0:T(2,128)(2,1)}, u32[]{:S(2)}) copy-start(bf16[176,2,768]{2,1,0:T(2,128)(2,1)} %weight.1) | copy-start | bytes 1622020

commit v3 on v2

--- a/solution.py
+++ b/solution.py
@@ -25,6 +25,7 @@
 MESH = pl.DeviceIdType.MESH
 TILE = 256
 STEP = 16
+PARTS = 4
 FAR = (4, 3, 5, 2, 6, 1, 7, 0)
 
 
@@ -104,9 +105,9 @@
 
 
 def kernel(
-    gradient, momentum, weight,
-    new_momentum, update, new_weight,
-    g_buf, m_buf, w_buf, nm_buf, advance, arrived, current, after, gram, poly, finished, returned, nw_buf,
+    gradient, momentum,
+    new_momentum, returned,
+    g_buf, m_buf, nm_buf, advance, arrived, current, after, gram, poly, finished,
     ready, load_sem, store_sem, own_sem, send_sem, recv_sem, back_send, back_recv,
 ):
     dp = lax.axis_index("dp")
@@ -122,7 +123,6 @@
     loads = [
         pltpu.make_async_copy(gradient, g_buf, load_sem.at[0]),
         pltpu.make_async_copy(momentum, m_buf, load_sem.at[1]),
-        pltpu.make_async_copy(weight, w_buf, load_sem.at[2]),
     ]
     for c in loads:
         c.start()
@@ -175,6 +175,8 @@
     @pl.when(core == 1)
     def _():
         pl.semaphore_wait(ready, 1)
+
+    slot = z * 64 + y * 8 + core * 4 + x
 
     def send_to(count, first, turn):
         @pl.loop(0, count)
@@ -192,7 +194,7 @@
                     @pl.when(jnp.logical_or(there != dp, x != tx))
                     def _():
                         pltpu.make_async_remote_copy(
-                            src_ref=advance.at[t], dst_ref=arrived.at[me], send_sem=send_sem, recv_sem=recv_sem,
+                            src_ref=advance.at[t], dst_ref=arrived.at[slot], send_sem=send_sem, recv_sem=recv_sem,
                             device_id=(there, tx), device_id_type=MESH,
                         ).start()
 
@@ -204,7 +206,7 @@
 
     @pl.when(owns)
     def _():
-        own = pltpu.make_async_copy(advance.at[mine], arrived.at[me], own_sem.at[0])
+        own = pltpu.make_async_copy(advance.at[mine], arrived.at[slot], own_sem.at[0])
         own.start()
         own.wait()
         pltpu.make_async_copy(
@@ -230,7 +232,7 @@
         groups = [lax.rem(x + dx, 4) for dx in (2, 1, 3, 0)]
 
         def finish(i, _):
-            plane = lax.rem(y + far_first(i), 8)
+            plane = lax.div(i, 4) * 4 + lax.rem(z + i, 4)
             r = pl.ds(pl.multiple_of(plane * 128, 128), 128)
             rows = after[r, :]
             product = jnp.dot(rows, poly[...], preferred_element_type=jnp.float32)
@@ -240,7 +242,9 @@
 
             @pl.loop(0, 8)
             def _(j):
-                there = (plane * 8 + lax.rem(z + far_first(j), 8)) * 2
+                ty = lax.rem(y + far_first(j), 8)
+                there = (ty * 8 + plane) * 2
+                row = plane * 64 + ty * 8
                 for way in range(8):
                     tx = groups[way % 4]
                     td = there + way // 4
@@ -248,14 +252,14 @@
                     @pl.when(jnp.logical_or(td != dp, tx != x))
                     def _():
                         pltpu.make_async_remote_copy(
-                            src_ref=finished.at[td * 4 + tx], dst_ref=returned.at[mine],
+                            src_ref=finished.at[row + way // 4 * 4 + tx], dst_ref=returned.at[mine],
                             send_sem=back_send, recv_sem=back_recv, device_id=(td, tx), device_id_type=MESH,
                         ).start()
 
             return 0
 
         lax.fori_loop(0, 8, finish, 0)
-        own_back = pltpu.make_async_copy(finished.at[me], returned.at[mine], own_sem.at[1])
+        own_back = pltpu.make_async_copy(finished.at[slot], returned.at[mine], own_sem.at[1])
         own_back.start()
         own_back.wait()
         pltpu.make_async_copy(
@@ -273,42 +277,62 @@
         pltpu.make_async_copy(advance, advance, send_sem).wait()
         pltpu.make_async_copy(returned, returned, back_recv).wait()
 
-    keep_update = pltpu.make_async_copy(returned, update, store_sem.at[1])
-    keep_update.start()
-
-    def step(i, _):
-        s = pl.ds(pl.multiple_of(i * STEP, STEP), STEP)
-        nw_buf[s] = (
-            (1.0 - learning_rate * weight_decay) * w_buf[s].astype(jnp.float32)
-            - learning_rate * returned[s].astype(jnp.float32)
-        ).astype(jnp.bfloat16)
-        return 0
-
-    lax.fori_loop(0, MATS // STEP, step, 0)
-    keep_weight = pltpu.make_async_copy(nw_buf, new_weight, store_sem.at[2])
-    keep_weight.start()
     keep_momentum.wait()
-    keep_update.wait()
-    keep_weight.wait()
+
+
+def last_step(new_momentum_in, update_in, weight, new_momentum, update, new_weight, u_buf, w_buf, nw_buf, nm_buf, part_sem):
+    size = MATS // PARTS
+    parts = [pl.ds(i * size, size) for i in range(PARTS)]
+    loads = [
+        (
+            pltpu.make_async_copy(update_in.at[p], u_buf.at[p], part_sem.at[0, i]),
+            pltpu.make_async_copy(weight.at[p], w_buf.at[p], part_sem.at[1, i]),
+        )
+        for i, p in enumerate(parts)
+    ]
+    for pair in loads:
+        for c in pair:
+            c.start()
+    keeps = [pltpu.make_async_copy(new_momentum_in.at[p], nm_buf.at[p], part_sem.at[4, i]) for i, p in enumerate(parts)]
+    for c in keeps:
+        c.start()
+    stores = []
+    for i, p in enumerate(parts):
+        for c in loads[i]:
+            c.wait()
+        stores.append(pltpu.make_async_copy(u_buf.at[p], update.at[p], part_sem.at[2, i]))
+        stores[-1].start()
+
+        def step(j, _):
+            s = pl.ds(pl.multiple_of(i * size + j * (size // 2), size // 2), size // 2)
+            nw_buf[s] = (
+                (1.0 - learning_rate * weight_decay) * w_buf[s].astype(jnp.float32)
+                - learning_rate * u_buf[s].astype(jnp.float32)
+            ).astype(jnp.bfloat16)
+            return 0
+
+        lax.fori_loop(0, 2, step, 0)
+        stores.append(pltpu.make_async_copy(nw_buf.at[p], new_weight.at[p], part_sem.at[3, i]))
+        stores[-1].start()
+        keeps[i].wait()
+        stores.append(pltpu.make_async_copy(nm_buf.at[p], new_momentum.at[p], part_sem.at[5, i]))
+        stores[-1].start()
+    for c in stores:
+        c.wait()
 
 
 def per_device(gradient, momentum, weight):
     shape = gradient.shape
     f32, bf16 = jnp.float32, jnp.bfloat16
     blocks = (DEVICES,) + shape[1:]
-    return pl.pallas_call(
+    new_momentum, update = pl.pallas_call(
         kernel,
-        out_shape=(
-            jax.ShapeDtypeStruct(shape, f32),
-            jax.ShapeDtypeStruct(shape, bf16),
-            jax.ShapeDtypeStruct(shape, bf16),
-        ),
-        in_specs=[pl.BlockSpec(memory_space=pltpu.HBM)] * 3,
-        out_specs=[pl.BlockSpec(memory_space=pl.ANY)] * 3,
+        out_shape=(jax.ShapeDtypeStruct(shape, f32), jax.ShapeDtypeStruct(shape, bf16)),
+        in_specs=[pl.BlockSpec(memory_space=pl.ANY)] * 2,
+        out_specs=[pl.BlockSpec(memory_space=pl.ANY)] * 2,
         scratch_shapes=[
             pltpu.VMEM(shape, f32),
             pltpu.VMEM(shape, f32),
-            pltpu.VMEM(shape, bf16),
             pltpu.VMEM(shape, f32),
             pltpu.VMEM(shape, bf16),
             pltpu.VMEM(blocks, bf16),
@@ -317,11 +341,9 @@
             pltpu.VMEM((COLS, COLS), bf16),
             pltpu.VMEM((COLS, COLS), bf16),
             pltpu.VMEM(blocks, bf16),
-            pltpu.VMEM(shape, bf16),
-            pltpu.VMEM(shape, bf16),
             pltpu.SemaphoreType.REGULAR,
-            pltpu.SemaphoreType.DMA((3,)),
-            pltpu.SemaphoreType.DMA((3,)),
+            pltpu.SemaphoreType.DMA((2,)),
+            pltpu.SemaphoreType.DMA((1,)),
             pltpu.SemaphoreType.DMA((2,)),
             pltpu.SemaphoreType.DMA,
             pltpu.SemaphoreType.DMA,
@@ -329,9 +351,22 @@
             pltpu.SemaphoreType.DMA,
         ],
         compiler_params=pltpu.CompilerParams(
-            collective_id=0, has_side_effects=True, vmem_limit_bytes=48 * 2**20
+            collective_id=0, has_side_effects=True, vmem_limit_bytes=60 * 2**20
         ),
-    )(gradient, momentum, weight)
+    )(gradient, momentum)
+    return pl.pallas_call(
+        last_step,
+        out_shape=(
+            jax.ShapeDtypeStruct(shape, f32),
+            jax.ShapeDtypeStruct(shape, bf16),
+            jax.ShapeDtypeStruct(shape, bf16),
+        ),
+        in_specs=[pl.BlockSpec(memory_space=pl.ANY)] * 3,
+        out_specs=[pl.BlockSpec(memory_space=pl.ANY)] * 3,
+        scratch_shapes=[pltpu.VMEM(shape, bf16)] * 3
+        + [pltpu.VMEM(shape, f32), pltpu.SemaphoreType.DMA((6, PARTS))],
+        compiler_params=pltpu.CompilerParams(vmem_limit_bytes=60 * 2**20),
+    )(new_momentum, update, weight)
 
 
 def solution(mesh):

time: 70.2 us -> 62.6 us (0.89)
  local copies, waits for them, and re-layouts: 6.09 us -> 0 us
  Pallas kernels: 63.2 us -> 61.8 us
    unnamed x9 -> x0, local copies, waits for them, and re-layouts: 6.09 us -> none
    pallas_call x1, Pallas kernels: 63.2 us -> 58.9 us  [per_device(): pl.pallas_call(kernel, out_shape=(jax.ShapeDtypeStruct(shape, f32), jax.S...]
    pallas_call x0 -> x1, Pallas kernels: none -> 2.87 us  [per_device(): pl.pallas_call(last_step, out_shape=(jax.ShapeDtypeStruct(shape, f32), ja...]
where the time goes in v3:
time: 62.6 us; the launch traced here: 62.4 us
  Pallas kernels  61.8 us (99%)
  between operations  0.64 us (1%)
    pallas_call x1, Pallas kernels, per_device(): pl.pallas_call(kernel, out_shape=(jax.ShapeDtypeStruct(shape, f32), jax.S...  58.9 us
    pallas_call x1, Pallas kernels, per_device(): pl.pallas_call(last_step, out_shape=(jax.ShapeDtypeStruct(shape, f32), ja...  2.87 us

profile of v3, /device:TPU:1, one launch (start us, length us, event | category | flops | bytes accessed | tf_op | source)
XLA Modules:
  0.0 62.4 jit_solution(16455200291190662637)
XLA Ops:
  0.6 58.9 %shard_map.58 = (f32[176,2,768]{2,1,0:T(2,128)}, bf16[176,2,768]{2,1,0:T(2,128)(2,1)}) custom-call(f32[176,2,768]{2,1,0:T(2,128)} %gradient.1, f32[176,2,768]{2,1,0:T(2,128)} %momentum.1), custom_call_target="tpu_custom_call" | custom-call | tf_op jit(solution)/shard_map/pallas_call | solution.py:328
  59.6 2.9 %shard_map.59 = (f32[176,2,768]{2,1,0:T(2,128)}, bf16[176,2,768]{2,1,0:T(2,128)(2,1)}, bf16[176,2,768]{2,1,0:T(2,128)(2,1)}) custom-call(f32[176,2,768]{2,1,0:T(2,128)} %get-tuple-element.5.new_momentum_in, bf16[176,2,768]{2,1,0:T(2,128)(2,1)} %get-tuple-element.6.update_in, bf16[176,2,768]{2,1,0:T(2,128)(2,1)} %weight.1), custom_call_target="tpu_custom_call" | custom-call | tf_op jit(solution)/shard_map/pallas_call | solution.py:357

commit v4 on v3

--- a/solution.py
+++ b/solution.py
@@ -242,7 +242,7 @@
 
             @pl.loop(0, 8)
             def _(j):
-                ty = lax.rem(y + far_first(j), 8)
+                ty = lax.div(j, 4) * 4 + lax.rem(y + j, 4)
                 there = (ty * 8 + plane) * 2
                 row = plane * 64 + ty * 8
                 for way in range(8):

time: 62.6 us -> 62 us (level)
  Pallas kernels: 61.8 us -> 60.8 us
    pallas_call x1, Pallas kernels: 58.9 us -> 58 us  [per_device(): pl.pallas_call(kernel, out_shape=(jax.ShapeDtypeStruct(shape, f32), jax.S...]
where the time goes in v4:
time: 62 us; the launch traced here: 61.5 us
  Pallas kernels  60.8 us (98%)
  between operations  0.64 us (1%)
    pallas_call x1, Pallas kernels, per_device(): pl.pallas_call(kernel, out_shape=(jax.ShapeDtypeStruct(shape, f32), jax.S...  58 us
    pallas_call x1, Pallas kernels, per_device(): pl.pallas_call(last_step, out_shape=(jax.ShapeDtypeStruct(shape, f32), ja...  2.87 us

profile of v4, /device:TPU:1, one launch (start us, length us, event | category | flops | bytes accessed | tf_op | source)
XLA Modules:
  0.0 61.5 jit_solution(17376038727086198147)
XLA Ops:
  0.6 58.0 %shard_map.58 = (f32[176,2,768]{2,1,0:T(2,128)}, bf16[176,2,768]{2,1,0:T(2,128)(2,1)}) custom-call(f32[176,2,768]{2,1,0:T(2,128)} %gradient.1, f32[176,2,768]{2,1,0:T(2,128)} %momentum.1), custom_call_target="tpu_custom_call" | custom-call | tf_op jit(solution)/shard_map/pallas_call | solution.py:328
  58.6 2.9 %shard_map.59 = (f32[176,2,768]{2,1,0:T(2,128)}, bf16[176,2,768]{2,1,0:T(2,128)(2,1)}, bf16[176,2,768]{2,1,0:T(2,128)(2,1)}) custom-call(f32[176,2,768]{2,1,0:T(2,128)} %get-tuple-element.5.new_momentum_in, bf16[176,2,768]{2,1,0:T(2,128)(2,1)} %get-tuple-element.6.update_in, bf16[176,2,768]{2,1,0:T(2,128)(2,1)} %weight.1), custom_call_target="tpu_custom_call" | custom-call | tf_op jit(solution)/shard_map/pallas_call | solution.py:357

commit v5 on v4

--- a/solution.py
+++ b/solution.py
@@ -137,12 +137,12 @@
 
         @pl.loop(0, 8)
         def _(j):
-            along = lax.rem(z + far_first(j), 8) * 2
+            along = lax.rem(z + far_first(7 - j), 8) * 2
             for plane in planes:
                 for tx in groups:
                     if plane is planes[-1] and tx is groups[-1]:
 
-                        @pl.when(j != 7)
+                        @pl.when(j != 0)
                         def _():
                             pl.semaphore_signal(
                                 barrier, inc=1, device_id=(plane + along, tx), device_id_type=MESH

time: 62 us -> 62.5 us (level)
  no operation moved by 1% of the time
where the time goes in v5:
time: 62.5 us; the launch traced here: 62 us
  Pallas kernels  61.4 us (98%)
  between operations  0.64 us (1%)
    pallas_call x1, Pallas kernels, per_device(): pl.pallas_call(kernel, out_shape=(jax.ShapeDtypeStruct(shape, f32), jax.S...  58.5 us
    pallas_call x1, Pallas kernels, per_device(): pl.pallas_call(last_step, out_shape=(jax.ShapeDtypeStruct(shape, f32), ja...  2.87 us

profile of v5, /device:TPU:1, one launch (start us, length us, event | category | flops | bytes accessed | tf_op | source)
XLA Modules:
  0.0 62.0 jit_solution(17763473703232670169)
XLA Ops:
  0.6 58.5 %shard_map.58 = (f32[176,2,768]{2,1,0:T(2,128)}, bf16[176,2,768]{2,1,0:T(2,128)(2,1)}) custom-call(f32[176,2,768]{2,1,0:T(2,128)} %gradient.1, f32[176,2,768]{2,1,0:T(2,128)} %momentum.1), custom_call_target="tpu_custom_call" | custom-call | tf_op jit(solution)/shard_map/pallas_call | solution.py:328
  59.1 2.9 %shard_map.59 = (f32[176,2,768]{2,1,0:T(2,128)}, bf16[176,2,768]{2,1,0:T(2,128)(2,1)}, bf16[176,2,768]{2,1,0:T(2,128)(2,1)}) custom-call(f32[176,2,768]{2,1,0:T(2,128)} %get-tuple-element.5.new_momentum_in, bf16[176,2,768]{2,1,0:T(2,128)(2,1)} %get-tuple-element.6.update_in, bf16[176,2,768]{2,1,0:T(2,128)(2,1)} %weight.1), custom_call_target="tpu_custom_call" | custom-call | tf_op jit(solution)/shard_map/pallas_call | solution.py:357
